TPU v7x, 256 devices: a whole 4x4x8 slice. The times are simulated.
256 devices in a mesh: pipe: 16 (over y, z_lo, core), expert: 16 (over z_hi, x).
Axes of the slice: x: 4, y: 4, z: 8 (z_hi: 4, z_lo: 2; z = z_hi * 2 + z_lo), core: 2. Of those that a mesh axis runs over, the one named last changes fastest.
Arguments:
- forward_input: bfloat16 [16, 1024, 3584], P('pipe', 'expert'), may hold values from -6 to 6
- forward_route: int32 [16, 1024, 1], P('pipe', 'expert'), may hold values from 0 to 1; in each aligned block of 64 rows (0 to 63, 64 to 127, ..., all dimensions but the last counted through in order) at most 34 rows name the same one
- forward_weight: float32 [16, 1024], P('pipe', 'expert'), may hold values from 0.25 to 1
- backward_grad: bfloat16 [16, 1024, 3584], P('pipe', 'expert'), may hold values from -6 to 6
- backward_route: int32 [16, 1024, 1], P('pipe', 'expert'), may hold values from 0 to 1; in each aligned block of 64 rows (0 to 63, 64 to 127, ..., all dimensions but the last counted through in order) at most 34 rows name the same one
- backward_weight: float32 [16, 1024], P('pipe', 'expert'), may hold values from 0.25 to 1
- saved_hidden: bfloat16 [16, 2, 16, 34, 2048], P('pipe', None, None, None, 'expert'), may hold values from -6 to 6
- gate_weight: bfloat16 [16, 3584, 2048], P('pipe', None, 'expert'), may hold values from -0.09375 to 0.09375
- up_weight: bfloat16 [16, 3584, 2048], P('pipe', None, 'expert'), may hold values from -0.09375 to 0.09375
- down_weight: bfloat16 [16, 2048, 3584], P('pipe', 'expert'), may hold values from -0.1875 to 0.1875
Outputs:
- forward_output: bfloat16 [16, 1024, 3584], P('pipe', 'expert')
- input_grad: bfloat16 [16, 1024, 3584], P('pipe', 'expert')
Inputs may be any that keep to these rules, and one draw needn't show every extreme that they name: `forward_route`: within each device's 64 tokens at most 34 choose any one expert; in some blocks one expert is chosen by exactly 34. `backward_route`: within each device's 64 tokens at most 34 choose any one expert; in some blocks one expert is chosen by exactly 34.
All inputs are finite; a program needn't handle non-finite values.
Results may differ from a plain program's by a relative error of at most 0.0064.
Values may be sent and summed in bfloat16 or wider, within the bound.
A program may use at most 128 MiB of HBM per device.

v0:
```python
import jax
import jax.numpy as jnp
from jax import lax
from jax.sharding import PartitionSpec as P

EXPERTS = 2
CAP = 34


def passed_along(block, axis, distance):
    devices = range(lax.axis_size(axis))
    route = [((i - distance) % len(devices), i) for i in devices]
    return lax.ppermute(block, axis, route)


def pick_rows(route, values):
    onehot = (route[:, None] == jnp.arange(EXPERTS, dtype=jnp.int32)[None, :]).astype(jnp.int32)
    before = jnp.cumsum(onehot, axis=0) - onehot
    slot_of = jnp.sum(before * onehot, axis=1)
    flat_slot = route * CAP + slot_of
    picker = (jnp.arange(EXPERTS * CAP, dtype=jnp.int32)[:, None] == flat_slot[None, :]).astype(
        jnp.bfloat16
    )
    picked = jnp.dot(picker, values, preferred_element_type=jnp.float32).astype(jnp.bfloat16)
    return (flat_slot, picked)


def expert_forward(token_rows, gate_local, up_local, down_local):
    gate_pre = jnp.dot(token_rows, gate_local, preferred_element_type=jnp.float32)
    up_pre = jnp.dot(token_rows, up_local, preferred_element_type=jnp.float32)
    hidden = (jax.nn.silu(gate_pre) * up_pre).astype(jnp.bfloat16)
    return jnp.dot(hidden, down_local, preferred_element_type=jnp.float32).astype(jnp.bfloat16)


def expert_backward(grad_rows_in, pre_gate, pre_up, gate_local, up_local, down_local):
    contract_last = (((1,), (1,)), ((), ()))
    grad_hidden = lax.dot_general(
        grad_rows_in, down_local, contract_last, preferred_element_type=jnp.float32
    )
    sigmoid_gate = jax.nn.sigmoid(pre_gate)
    grad_gate = (
        grad_hidden * pre_up * sigmoid_gate * (1.0 + pre_gate * (1.0 - sigmoid_gate))
    ).astype(jnp.bfloat16)
    grad_up = (grad_hidden * pre_gate * sigmoid_gate).astype(jnp.bfloat16)
    partial_value = lax.dot_general(
        grad_gate, gate_local, contract_last, preferred_element_type=jnp.float32
    )
    partial_value = partial_value + lax.dot_general(
        grad_up, up_local, contract_last, preferred_element_type=jnp.float32
    )
    return partial_value.astype(jnp.bfloat16)


def move_rows(blocks):
    return lax.all_to_all(blocks, "expert", split_axis=0, concat_axis=0, tiled=True)


def per_device(
    forward_input,
    forward_route,
    forward_weight,
    backward_grad,
    backward_route,
    backward_weight,
    saved_hidden,
    gate_weight,
    up_weight,
    down_weight,
):
    holders = lax.axis_size("expert")
    shards = holders // EXPERTS
    features = forward_input.shape[2]
    rows_total = holders * CAP
    gate_local = gate_weight[0]
    up_local = up_weight[0]
    down_local = down_weight[0]
    flat_fwd, rows_fwd = pick_rows(forward_route[0, :, 0], forward_input[0])
    scaled = (backward_weight[0][:, None] * backward_grad[0].astype(jnp.float32)).astype(
        jnp.bfloat16
    )
    flat_bwd, rows_bwd = pick_rows(backward_route[0, :, 0], scaled)
    pre_gate = saved_hidden[0, 0].reshape(rows_total, -1).astype(jnp.float32)
    pre_up = saved_hidden[0, 1].reshape(rows_total, -1).astype(jnp.float32)
    received_fwd = move_rows(
        jnp.repeat(rows_fwd.reshape(EXPERTS, 1, CAP, features), shards, axis=0)
    )
    partial_fwd = expert_forward(
        received_fwd.reshape(rows_total, features), gate_local, up_local, down_local
    )
    sums_fwd = move_rows(partial_fwd.reshape(holders, 1, CAP, features))[:, 0]
    received_bwd = move_rows(
        jnp.repeat(rows_bwd.reshape(EXPERTS, 1, CAP, features), shards, axis=0)
    )
    partial_bwd = expert_backward(
        received_bwd.reshape(rows_total, features),
        pre_gate,
        pre_up,
        gate_local,
        up_local,
        down_local,
    )
    sums_bwd = move_rows(partial_bwd.reshape(holders, 1, CAP, features))[:, 0]
    total_fwd = jnp.sum(
        sums_fwd.astype(jnp.float32).reshape(EXPERTS, shards, CAP, features), axis=1
    )
    total_bwd = jnp.sum(
        sums_bwd.astype(jnp.float32).reshape(EXPERTS, shards, CAP, features), axis=1
    )
    total_fwd = total_fwd.reshape(EXPERTS * CAP, features)
    total_bwd = total_bwd.reshape(EXPERTS * CAP, features)
    forward_token = (forward_weight[0][:, None] * jnp.take(total_fwd, flat_fwd, axis=0)).astype(
        jnp.bfloat16
    )
    grad_token = jnp.take(total_bwd, flat_bwd, axis=0).astype(jnp.bfloat16)
    forward_next = passed_along(forward_token, "pipe", 1)
    grad_before = passed_along(grad_token, "pipe", -1)
    return (forward_next[None], grad_before[None])


def solution(mesh):
    placed = (
        P("pipe", "expert", None),
        P("pipe", "expert", None),
        P("pipe", "expert"),
        P("pipe", "expert", None),
        P("pipe", "expert", None),
        P("pipe", "expert"),
        P("pipe", None, None, None, "expert"),
        P("pipe", None, "expert"),
        P("pipe", None, "expert"),
        P("pipe", "expert", None),
    )
    return jax.shard_map(
        per_device,
        mesh=mesh,
        in_specs=placed,
        out_specs=(P("pipe", "expert", None), P("pipe", "expert", None)),
        check_vma=False,
    )
```

profile of v0, /device:TPU:4, one launch (start us, length us, event | category | flops | bytes accessed | tf_op | source)
XLA Modules:
  0.0 525.2 jit_solution(11366876868105801494)
XLA Ops:
  0.6 0.8 fusion.25
  1.5 0.8 select_reduce_fusion
  2.4 0.7 compare_and_fusion
  3.1 1.4 convolution_convert_fusion.1
  4.6 2.4 broadcast_in_dim.34
  7.0 11.6 %all-to-all-start.2 = ((bf16[16,1,34,3584]{3,2,1,0:T(8,128)(2,1)}), bf16[16,1,34,3584]{3,2,1,0:T(8,128)(2,1)}, u32[]{:S(2)}, u32[]{:S(2)}) async-start(bf16[16,1,34,3584]{3,2,1,0:T(8,128)(2,1)} %bitcast.52), calls=%async_computation.2 | async-start | bytes 9175040 | tf_op jit(solution)/shard_map/all_to_all | solution.py:55
  19.9 102.3 %all-to-all-done.2 = bf16[16,1,34,3584]{3,2,1,0:T(8,128)(2,1)} async-done(((bf16[16,1,34,3584]{3,2,1,0:T(8,128)(2,1)}), bf16[16,1,34,3584]{3,2,1,0:T(8,128)(2,1)}, u32[]{:S(2)}, u32[]{:S(2)}) %all-to-all-start.2) | async-done | bytes 3899424 | tf_op jit(solution)/shard_map/all_to_all | solution.py:55
  122.2 2.5 broadcast_in_dim.31
  124.8 5.8 %all-to-all-start = ((bf16[16,1,34,3584]{3,2,1,0:T(8,128)(2,1)}), bf16[16,1,34,3584]{3,2,1,0:T(8,128)(2,1)}, u32[]{:S(2)}, u32[]{:S(2)}) async-start(bf16[16,1,34,3584]{3,2,1,0:T(8,128)(2,1)} %bitcast.51), calls=%async_computation | async-start | bytes 9175040 | tf_op jit(solution)/shard_map/all_to_all | solution.py:55
  130.9 5.2 reshape.84
  136.1 3.3 fusion.2
  139.5 1.2 fusion.8
  140.7 3.0 add_convert_fusion
  143.7 5.2 reshape.85
  149.0 58.3 %all-to-all-done = bf16[16,1,34,3584]{3,2,1,0:T(8,128)(2,1)} async-done(((bf16[16,1,34,3584]{3,2,1,0:T(8,128)(2,1)}), bf16[16,1,34,3584]{3,2,1,0:T(8,128)(2,1)}, u32[]{:S(2)}, u32[]{:S(2)}) %all-to-all-start) | async-done | bytes 3899424 | tf_op jit(solution)/shard_map/all_to_all | solution.py:55
  207.2 22.5 %all-to-all-start.3 = ((bf16[16,1,34,3584]{3,2,1,0:T(8,128)(2,1)}), bf16[16,1,34,3584]{3,2,1,0:T(8,128)(2,1)}, u32[]{:S(2)}, u32[]{:S(2)}) async-start(bf16[16,1,34,3584]{3,2,1,0:T(8,128)(2,1)} %bitcast.53), calls=%async_computation.3 | async-start | bytes 9175040 | tf_op jit(solution)/shard_map/all_to_all | solution.py:55
  229.7 5.1 reshape.80
  234.9 3.3 fusion.10
  238.1 8.1 %convolution_convert_fusion = bf16[544,3584]{1,0:T(8,128)(2,1)} fusion(bf16[544,3584]{1,0:T(8,128)(2,1)} %reshape.80, bf16[1,128,3584]{2,1,0:T(8,128)(2,1)S(1)} %copy-done.2, bf16[1,3584,128]{2,1,0:T(8,128)(2,1)S(1)} %copy-done, f32[544,128]{1,0:T(8,128)S(1)} %fusion.10), kind=kOutput, calls=%fused_computation.5 | convolution fusion | flops 1000611840 | bytes 9912320 | tf_op jit(solution)/shard_map/dot_general | solution.py:32
  246.3 5.1 reshape.81
  251.4 57.6 %all-to-all-done.3 = bf16[16,1,34,3584]{3,2,1,0:T(8,128)(2,1)} async-done(((bf16[16,1,34,3584]{3,2,1,0:T(8,128)(2,1)}), bf16[16,1,34,3584]{3,2,1,0:T(8,128)(2,1)}, u32[]{:S(2)}, u32[]{:S(2)}) %all-to-all-start.3) | async-done | bytes 3899424 | tf_op jit(solution)/shard_map/all_to_all | solution.py:55
  309.0 9.9 %all-to-all-start.1 = ((bf16[16,1,34,3584]{3,2,1,0:T(8,128)(2,1)}), bf16[16,1,34,3584]{3,2,1,0:T(8,128)(2,1)}, u32[]{:S(2)}, u32[]{:S(2)}) async-start(bf16[16,1,34,3584]{3,2,1,0:T(8,128)(2,1)} %bitcast.50), calls=%async_computation.1 | async-start | bytes 9175040 | tf_op jit(solution)/shard_map/all_to_all | solution.py:55
  319.5 3.0 convert_reduce_fusion
  322.6 0.8 gather_fusion.1
  323.5 0.9 select_convert_fusion
  324.4 115.5 %collective-permute-start.1 = (bf16[64,3584]{1,0:T(8,128)(2,1)}, bf16[64,3584]{1,0:T(8,128)(2,1)S(1)}, u32[]{:S(2)}, u32[]{:S(2)}) collective-permute-start(bf16[64,3584]{1,0:T(8,128)(2,1)} %select_convert_fusion), channel_id=1, source_target_pairs={{16,0},{32,16},{48,32},{64,48},{80,64},{96,80},{112,96},{128,112},... | collective-permute-start | bytes 1376264 | tf_op jit(solution)/shard_map/ppermute | solution.py:13
  439.9 3.1 convert_reduce_fusion.1
  443.2 1.1 gather_fusion
  444.6 14.2 %collective-permute-done.1 = bf16[64,3584]{1,0:T(8,128)(2,1)S(1)} collective-permute-done((bf16[64,3584]{1,0:T(8,128)(2,1)}, bf16[64,3584]{1,0:T(8,128)(2,1)S(1)}, u32[]{:S(2)}, u32[]{:S(2)}) %collective-permute-start.1) | collective-permute-done | bytes 458784 | tf_op jit(solution)/shard_map/ppermute | solution.py:13
  458.8 64.9 %collective-permute-done = bf16[64,3584]{1,0:T(8,128)(2,1)S(1)} collective-permute-done((bf16[64,3584]{1,0:T(8,128)(2,1)S(1)}, bf16[64,3584]{1,0:T(8,128)(2,1)S(1)}, u32[]{:S(2)}, u32[]{:S(2)}) %collective-permute-start) | collective-permute-done | bytes 458784 | tf_op jit(solution)/shard_map/ppermute | solution.py:13
  523.7 0.8 copy.22
  524.5 0.8 copy.23
  (38 shorter events, 2.9 us)
Async XLA Ops:
  0.6 140.0 %copy-start = (bf16[1,3584,128]{2,1,0:T(8,128)(2,1)S(1)}, bf16[1,3584,128]{2,1,0:T(8,128)(2,1)}, u32[]{:S(2)}) copy-start(bf16[1,3584,128]{2,1,0:T(8,128)(2,1)} %param.20) | copy-start | bytes 2752516
  6.9 11.6 %copy-start.5 = (s32[1,64,1]{1,2,0:T(1,128)S(1)}, s32[1,64,1]{1,2,0:T(1,128)}, u32[]{:S(2)}) copy-start(s32[1,64,1]{1,2,0:T(1,128)} %param.13) | copy-start | bytes 772
  7.0 12.5 %copy-start.3 = (bf16[1,64,3584]{2,1,0:T(8,128)(2,1)S(1)}, bf16[1,64,3584]{2,1,0:T(8,128)(2,1)}, u32[]{:S(2)}) copy-start(bf16[1,64,3584]{2,1,0:T(8,128)(2,1)} %param.12) | copy-start | bytes 1376260
  7.0 115.3 %all-to-all-start.2 = ((bf16[16,1,34,3584]{3,2,1,0:T(8,128)(2,1)}), bf16[16,1,34,3584]{3,2,1,0:T(8,128)(2,1)}, u32[]{:S(2)}, u32[]{:S(2)}) async-start(bf16[16,1,34,3584]{3,2,1,0:T(8,128)(2,1)} %bitcast.52), calls=%async_computation.2 | async-start | bytes 9175040 | tf_op jit(solution)/shard_map/all_to_all | solution.py:55
  124.8 5.8 %copy-start.4 = (bf16[1,2,16,34,128]{4,2,3,1,0:T(8,128)(2,1)S(1)}, bf16[1,2,16,34,128]{4,2,3,1,0:T(8,128)(2,1)}, u32[]{:S(2)}) copy-start(bf16[1,2,16,34,128]{4,2,3,1,0:T(8,128)(2,1)} %param.18) | copy-start | bytes 835588
  124.8 82.5 %all-to-all-start = ((bf16[16,1,34,3584]{3,2,1,0:T(8,128)(2,1)}), bf16[16,1,34,3584]{3,2,1,0:T(8,128)(2,1)}, u32[]{:S(2)}, u32[]{:S(2)}) async-start(bf16[16,1,34,3584]{3,2,1,0:T(8,128)(2,1)} %bitcast.51), calls=%async_computation | async-start | bytes 9175040 | tf_op jit(solution)/shard_map/all_to_all | solution.py:55
  130.8 5.3 %copy-start.2 = (bf16[1,128,3584]{2,1,0:T(8,128)(2,1)S(1)}, bf16[1,128,3584]{2,1,0:T(8,128)(2,1)}, u32[]{:S(2)}) copy-start(bf16[1,128,3584]{2,1,0:T(8,128)(2,1)} %param.21) | copy-start | bytes 2752516
  136.1 3.4 copy-start.1
  207.2 101.8 %all-to-all-start.3 = ((bf16[16,1,34,3584]{3,2,1,0:T(8,128)(2,1)}), bf16[16,1,34,3584]{3,2,1,0:T(8,128)(2,1)}, u32[]{:S(2)}, u32[]{:S(2)}) async-start(bf16[16,1,34,3584]{3,2,1,0:T(8,128)(2,1)} %bitcast.53), calls=%async_computation.3 | async-start | bytes 9175040 | tf_op jit(solution)/shard_map/all_to_all | solution.py:55
  309.0 130.9 %all-to-all-start.1 = ((bf16[16,1,34,3584]{3,2,1,0:T(8,128)(2,1)}), bf16[16,1,34,3584]{3,2,1,0:T(8,128)(2,1)}, u32[]{:S(2)}, u32[]{:S(2)}) async-start(bf16[16,1,34,3584]{3,2,1,0:T(8,128)(2,1)} %bitcast.50), calls=%async_computation.1 | async-start | bytes 9175040 | tf_op jit(solution)/shard_map/all_to_all | solution.py:55
  324.4 134.4 %collective-permute-start.1 = (bf16[64,3584]{1,0:T(8,128)(2,1)}, bf16[64,3584]{1,0:T(8,128)(2,1)S(1)}, u32[]{:S(2)}, u32[]{:S(2)}) collective-permute-start(bf16[64,3584]{1,0:T(8,128)(2,1)} %select_convert_fusion), channel_id=1, source_target_pairs={{16,0},{32,16},{48,32},{64,48},{80,64},{96,80},{112,96},{128,112},... | collective-permute-start | bytes 1376264 | tf_op jit(solution)/shard_map/ppermute | solution.py:13
  443.1 1.2 copy-start.6
  443.1 1.2 copy-start.7
  444.5 79.2 %collective-permute-start = (bf16[64,3584]{1,0:T(8,128)(2,1)S(1)}, bf16[64,3584]{1,0:T(8,128)(2,1)S(1)}, u32[]{:S(2)}, u32[]{:S(2)}) collective-permute-start(bf16[64,3584]{1,0:T(8,128)(2,1)S(1)} %fusion.12), channel_id=1, source_target_pairs={{240,0},{0,16},{16,32},{32,48},{48,64},{64,80},{80,96},{96,112},{1... | collective-permute-start | bytes 1376264 | tf_op jit(solution)/shard_map/ppermute | solution.py:13
where the time goes:
time: 526 us; the launch traced here: 525 us
  waiting for transfers between devices  297 us (56%)
  starting transfers between devices  165 us (31%)
  local copies, waits for them, and re-layouts  29.9 us (6%)
  matrix products  20.6 us (4%)
  other arithmetic  11.1 us (2%)
    all_to_all x4, waiting for transfers between devices, move_rows(): lax.all_to_all(blocks, 'expert', split_axis=0, concat_axis=0, tiled=True)  218 us
    ppermute x2, starting transfers between devices, passed_along(): return lax.ppermute(block, axis, route)  116 us
    ppermute x2, waiting for transfers between devices, passed_along(): return lax.ppermute(block, axis, route)  79.1 us
    all_to_all x4, starting transfers between devices, move_rows(): lax.all_to_all(blocks, 'expert', split_axis=0, concat_axis=0, tiled=True)  49.7 us
  transfers between devices with their start and end apart: 6, of which 5 were waited for; matrix products, arithmetic and copies ran while one was open for 10% of the time, Pallas kernels for 0%

commit v1 on v0

v1 whole, which is shorter than its diff:
```python
import jax
import jax.numpy as jnp
from jax import lax
from jax.experimental import pallas as pl
from jax.experimental.pallas import tpu as pltpu
from jax.sharding import PartitionSpec as P

MESH = pl.DeviceIdType.MESH
BF16 = jnp.bfloat16
F32 = jnp.float32
CAP = 34
TOK = 64
D = 3584
UNITS = 128
BLK = 512
NBLK = D // BLK
GROUPS = ((0, 2), (2, 4), (4, 6), (6, 7))
NG = len(GROUPS)
FWD, BWD = 0, 1


def iota(shape, dim):
    return lax.broadcasted_iota(jnp.int32, shape, dim)


def dot(a, b):
    return jnp.dot(a, b, preferred_element_type=F32)


def dot_t(a, b):
    return lax.dot_general(a, b, (((1,), (1,)), ((), ())), preferred_element_type=F32)


def group_cols(g):
    first, last = GROUPS[g]
    return pl.ds(first * BLK, (last - first) * BLK)


def block_cols(c):
    return pl.ds(c * BLK, BLK)


def row_index(route):
    route = jnp.broadcast_to(route, (TOK, 128))
    to_one = (route == 1).astype(F32)
    earlier = (iota((TOK, TOK), 1) < iota((TOK, TOK), 0)).astype(BF16)
    ones_before = dot(earlier, to_one.astype(BF16))
    place = iota((TOK, 128), 0).astype(F32)
    return jnp.where(route == 1, CAP + ones_before, place - ones_before)


def tokens_in_lanes(index):
    diagonal = iota((TOK, TOK), 0) == iota((TOK, TOK), 1)
    spread = jnp.where(diagonal, index[:, :TOK], 0.0).astype(BF16)
    return dot(jnp.ones((TOK, TOK), BF16), spread)


def unpack_extra(c):
    row, col = iota((16, 128), 0), iota((16, 128), 1)
    return (((col >> 4) == (row >> 1)) & ((col & 15) == 2 * c + (row & 1))).astype(BF16)


def pack_extra(c):
    row, col = iota((128, 16), 0), iota((128, 16), 1)
    return (((row >> 4) == (col >> 1)) & ((row & 15) == 2 * c + (col & 1))).astype(BF16)


def kernel(
    fi, fr, fw, bg, br, bw, saved, gate, up, down,
    out_f, out_b,
    gw, uw, dw, sv,
    ds_main, ds_extra, tok, tok_extra,
    info_s, info_r,
    acc_a, acc_b, act_a, act_b,
    own, own_extra,
    xs, xs_extra, xr, xr_extra,
    zs, zs_extra, zr, zr_extra,
    loc_sem,
    w_send, w_recv, i_send, i_recv,
    zd_send, zd_recv, xd_send, xd_recv,
    xc_send, xc_recv, zc_send, zc_recv,
):
    p = lax.axis_index("pipe")
    e = lax.axis_index("expert")
    z, x = e // 4, e % 4
    turn = 1 - 2 * ((x + p) % 2)
    x_w = (x + turn + 4) % 4
    x_t = (x - turn + 4) % 4
    x_far = (x + 2) % 4
    weight_peer = (p, z * 4 + x_w)
    token_peer = (p, z * 4 + x_t)
    after, before = (p + 1) % 16, (p + 15) % 16

    barrier = pltpu.get_barrier_semaphore()
    peers = [weight_peer, token_peer]
    peers += [(p, ((z + dz) % 4) * 4 + x) for dz in range(1, 4)]
    peers += [(q, ((z + dz) % 4) * 4 + x) for q in (after, before) for dz in range(4)]
    for peer in peers:
        pl.semaphore_signal(barrier, inc=1, device_id=peer, device_id_type=MESH)

    sends = []

    def remote(src, dst, send, recv, peer):
        copy = pltpu.make_async_remote_copy(
            src_ref=src, dst_ref=dst, send_sem=send, recv_sem=recv,
            device_id=peer, device_id_type=MESH,
        )
        copy.start()
        sends.append(copy)
        return copy

    local = [
        pltpu.make_async_copy(gate.at[0], gw.at[:, pl.ds(0, UNITS)], loc_sem.at[0]),
        pltpu.make_async_copy(up.at[0], uw.at[:, pl.ds(0, UNITS)], loc_sem.at[1]),
        pltpu.make_async_copy(down.at[0], dw.at[pl.ds(0, UNITS)], loc_sem.at[2]),
        pltpu.make_async_copy(saved.at[:, :, x], sv.at[0, 0], loc_sem.at[3]),
        pltpu.make_async_copy(saved.at[:, :, x_t], sv.at[0, 1], loc_sem.at[4]),
    ]
    for copy in local:
        copy.start()

    index_f = row_index(fr[0])
    index_b = row_index(br[0])
    info_s[BWD] = index_b
    weight_spread = jnp.where(
        iota((TOK, TOK), 0) == iota((TOK, TOK), 1), jnp.broadcast_to(fw[...], (TOK, TOK)), 0.0
    )
    weight_col = jnp.sum(weight_spread, axis=1, keepdims=True)
    info_s[FWD] = jnp.where(
        iota((TOK, 128), 1) == 1, jnp.broadcast_to(weight_col, (TOK, 128)), index_f
    )
    grad_spread = jnp.where(
        iota((TOK, TOK), 0) == iota((TOK, TOK), 1), jnp.broadcast_to(bw[...], (TOK, TOK)), 0.0
    )
    grad_col = jnp.sum(grad_spread, axis=1, keepdims=True)

    def pick(mb, index, read):
        by_lane = tokens_in_lanes(index)
        row = iota((TOK, TOK), 0)
        picker = (by_lane == ((row >> 5) * CAP + (row & 31)).astype(F32)).astype(BF16)
        row = iota((32, TOK), 0)
        extra_id = (row >> 4) * CAP + 32 + (row & 1)
        extra = jnp.zeros((32, BLK), F32)
        for c in range(NBLK):
            values = read(c)
            picked = dot(picker, values).astype(BF16)
            ds_main[mb, 0, :, block_cols(c)] = picked[:32]
            ds_main[mb, 1, :, block_cols(c)] = picked[32:]
            wanted = jnp.where(((row & 15) >> 1) == c, extra_id, -1).astype(F32)
            extra += dot((by_lane[:32] == wanted).astype(BF16), values)
        extra = extra.astype(BF16)
        ds_extra[mb, 0] = extra[:16]
        ds_extra[mb, 1] = extra[16:]
        tok[mb, 0, z] = ds_main[mb, z // 2]
        tok_extra[mb, 0, z] = ds_extra[mb, z // 2]

    def read_grad(c):
        return (grad_col * bg[0, :, block_cols(c)].astype(F32)).astype(BF16)

    def read_input(c):
        return fi[0, :, block_cols(c)]

    zd = {}
    xd = {}

    def send_rows(mb):
        for g in (NG, *range(NG)):
            for dz in (2, 1, 3):
                tz = (z + dz) % 4
                if g == NG:
                    src, dst = ds_extra.at[mb, tz // 2], tok_extra.at[mb, 0, z]
                else:
                    src = ds_main.at[mb, tz // 2, :, group_cols(g)]
                    dst = tok.at[mb, 0, z, :, group_cols(g)]
                zd[mb, g, dz] = remote(
                    src, dst, zd_send.at[mb, g, dz - 1], zd_recv.at[mb, g, dz - 1],
                    (p, tz * 4 + x),
                )

    def pass_rows(mb, g):
        for dz in range(1, 4):
            zd[mb, g, dz].wait_recv()
        if g == NG:
            src, dst = tok_extra.at[mb, 0], tok_extra.at[mb, 1]
        else:
            src = tok.at[mb, 0, :, :, group_cols(g)]
            dst = tok.at[mb, 1, :, :, group_cols(g)]
        xd[mb, g] = remote(src, dst, xd_send.at[mb, g], xd_recv.at[mb, g], token_peer)

    pick(BWD, index_b, read_grad)
    pl.semaphore_wait(barrier, len(peers))

    from_down = remote(down.at[0], dw.at[pl.ds(UNITS, UNITS)], w_send.at[0], w_recv.at[0], weight_peer)
    from_saved = [
        remote(saved.at[:, :, x_w], sv.at[1, 0], w_send.at[1], w_recv.at[1], weight_peer),
        remote(saved.at[:, :, x_far], sv.at[1, 1], w_send.at[2], w_recv.at[2], weight_peer),
    ]
    send_rows(BWD)
    infos = [
        remote(info_s.at[FWD], info_r.at[FWD], i_send.at[FWD], i_recv.at[FWD], (after, e)),
        remote(info_s.at[BWD], info_r.at[BWD], i_send.at[BWD], i_recv.at[BWD], (before, e)),
    ]
    pick(FWD, index_f, read_input)
    send_rows(FWD)

    for g in (NG, *range(NG)):
        pass_rows(BWD, g)

    from_gate, from_up = [], []
    for g in range(NG):
        cols = group_cols(g)
        from_gate.append(remote(
            gate.at[0, cols], gw.at[cols, pl.ds(UNITS, UNITS)], w_send.at[3 + g], w_recv.at[3 + g], weight_peer))
        from_up.append(remote(
            up.at[0, cols], uw.at[cols, pl.ds(UNITS, UNITS)], w_send.at[3 + NG + g], w_recv.at[3 + NG + g], weight_peer))

    def rows_of(mb, c):
        main = tok[mb, :, :, :, block_cols(c)].reshape(256, BLK)
        extra = dot(unpack_extra(c), tok_extra[mb].reshape(128, BLK)).astype(BF16)
        return jnp.concatenate([main, extra], axis=0)

    for copy in local:
        copy.wait()
    from_down.wait_recv()
    acc_a[...] = jnp.zeros_like(acc_a)
    xd[BWD, NG].wait_recv()
    for g in range(NG):
        xd[BWD, g].wait_recv()
        for c in range(*GROUPS[g]):
            acc_a[...] += dot_t(rows_of(BWD, c), dw[:, block_cols(c)])
    for copy in from_saved:
        copy.wait_recv()

    def saved_rows(kind, h):
        main = sv[h, :, kind, :, 0:32, :].reshape(256, UNITS).astype(F32)
        extra = [sv[h, w, kind, s, 32:34, :].astype(F32) for w in range(2) for s in range(4)]
        return jnp.concatenate([main, *extra], axis=0)

    for h in range(2):
        lanes = pl.ds(h * UNITS, UNITS)
        g_pre, u_pre = saved_rows(0, h), saved_rows(1, h)
        sig = jax.nn.sigmoid(g_pre)
        grad = acc_a[:, lanes]
        act_a[:, lanes] = (grad * u_pre * sig * (1.0 + g_pre * (1.0 - sig))).astype(BF16)
        act_b[:, lanes] = (grad * g_pre * sig).astype(BF16)

    xc, zc = {}, {}

    def keep(mb, c, value):
        own[:, block_cols(c)] = value[:128]
        xs[mb, :, :, block_cols(c)] = value[128:256].astype(BF16).reshape(4, 32, BLK)
        own_extra[...] += dot(pack_extra(c), value[256:].astype(BF16))

    def send_part(mb, g):
        if g == NG:
            xs_extra[mb] = own_extra[64:].astype(BF16).reshape(4, 16, BLK)
            src, dst = xs_extra.at[mb], xr_extra.at[mb]
        else:
            src, dst = xs.at[mb, :, :, group_cols(g)], xr.at[mb, :, :, group_cols(g)]
        xc[mb, g] = remote(src, dst, xc_send.at[mb, g], xc_recv.at[mb, g], token_peer)

    def send_sum(mb, g):
        section = after if mb == FWD else before
        xc[mb, g].wait_recv()
        if g == NG:
            zs_extra[mb] = (own_extra[:64].reshape(4, 16, BLK) + xr_extra[mb].astype(F32)).astype(BF16)
        else:
            for c in range(*GROUPS[g]):
                cols = block_cols(c)
                zs[mb, :, :, cols] = (
                    own[:, cols].reshape(4, 32, BLK) + xr[mb, :, :, cols].astype(F32)
                ).astype(BF16)
        for dz in (2, 1, 3, 0):
            tz = (z + dz) % 4
            if g == NG:
                src, dst = zs_extra.at[mb, tz], zr_extra.at[mb, z]
            else:
                src, dst = zs.at[mb, tz, :, group_cols(g)], zr.at[mb, z, :, group_cols(g)]
            zc[mb, g, dz] = remote(
                src, dst, zc_send.at[mb, g, dz], zc_recv.at[mb, g, dz], (section, tz * 4 + x))

    own_extra[...] = jnp.zeros_like(own_extra)
    pass_rows(FWD, NG)
    for g in range(NG):
        pass_rows(FWD, g)
        from_gate[g].wait_recv()
        from_up[g].wait_recv()
        for c in range(*GROUPS[g]):
            rows = block_cols(c)
            keep(BWD, c, dot_t(act_a[...], gw[rows]) + dot_t(act_b[...], uw[rows]))
        send_part(BWD, g)
        if g > 0:
            send_sum(BWD, g - 1)
    send_part(BWD, NG)
    send_sum(BWD, NG - 1)
    send_sum(BWD, NG)

    acc_a[...] = jnp.zeros_like(acc_a)
    acc_b[...] = jnp.zeros_like(acc_b)
    xd[FWD, NG].wait_recv()
    for g in range(NG):
        xd[FWD, g].wait_recv()
        for c in range(*GROUPS[g]):
            rows = rows_of(FWD, c)
            acc_a[...] += dot(rows, gw[block_cols(c)])
            acc_b[...] += dot(rows, uw[block_cols(c)])
    act_a[...] = (jax.nn.silu(acc_a[...]) * acc_b[...]).astype(BF16)
    own_extra[...] = jnp.zeros_like(own_extra)
    for g in range(NG):
        for c in range(*GROUPS[g]):
            keep(FWD, c, dot(act_a[...], dw[:, block_cols(c)]))
        send_part(FWD, g)
        if g > 0:
            send_sum(FWD, g - 1)
    send_part(FWD, NG)
    send_sum(FWD, NG - 1)
    send_sum(FWD, NG)

    def place(mb, out):
        infos[mb].wait_recv()
        info = info_r[mb]
        index = info[:, 0:1]
        col = iota((TOK, 128), 1)
        whole = (index == ((col >> 6) * CAP + (col & 31)).astype(F32)).astype(BF16)
        col = iota((TOK, TOK), 1)
        extra_id = (col >> 5) * CAP + 32 + (col & 1)
        for g in (NG, *range(NG)):
            for dz in range(4):
                zc[mb, g, dz].wait_recv()
            if g == NG:
                continue
            for c in range(*GROUPS[g]):
                wanted = jnp.where(((col & 15) >> 1) == c, extra_id, -1).astype(F32)
                value = dot(whole, zr[mb, :, :, block_cols(c)].reshape(128, BLK))
                value += dot((index == wanted).astype(BF16), zr_extra[mb].reshape(64, BLK))
                if mb == FWD:
                    value = info[:, 1:2] * value
                out[0, :, block_cols(c)] = value.astype(BF16)

    place(BWD, out_b)
    place(FWD, out_f)
    for copy in sends:
        copy.wait_send()


def per_device(fi, fr, fw, bg, br, bw, saved, gate, up, down):
    vmem = pl.BlockSpec(memory_space=pltpu.VMEM)
    anywhere = pl.BlockSpec(memory_space=pl.ANY)
    dma = pltpu.SemaphoreType.DMA
    rows_out = jax.ShapeDtypeStruct((1, TOK, D), BF16)
    saved = saved[0].reshape(2, 4, 4, CAP, UNITS)
    return pl.pallas_call(
        kernel,
        out_shape=(rows_out, rows_out),
        in_specs=[vmem] * 6 + [anywhere] * 4,
        out_specs=(vmem, vmem),
        scratch_shapes=[
            pltpu.VMEM((D, 2 * UNITS), BF16),
            pltpu.VMEM((D, 2 * UNITS), BF16),
            pltpu.VMEM((2 * UNITS, D), BF16),
            pltpu.VMEM((2, 2, 2, 4, CAP, UNITS), BF16),
            pltpu.VMEM((2, 2, 32, D), BF16),
            pltpu.VMEM((2, 2, 16, BLK), BF16),
            pltpu.VMEM((2, 2, 4, 32, D), BF16),
            pltpu.VMEM((2, 2, 4, 16, BLK), BF16),
            pltpu.VMEM((2, TOK, 128), F32),
            pltpu.VMEM((2, TOK, 128), F32),
            pltpu.VMEM((272, 256), F32),
            pltpu.VMEM((272, 256), F32),
            pltpu.VMEM((272, 256), BF16),
            pltpu.VMEM((272, 256), BF16),
            pltpu.VMEM((128, D), F32),
            pltpu.VMEM((128, BLK), F32),
            pltpu.VMEM((2, 4, 32, D), BF16),
            pltpu.VMEM((2, 4, 16, BLK), BF16),
            pltpu.VMEM((2, 4, 32, D), BF16),
            pltpu.VMEM((2, 4, 16, BLK), BF16),
            pltpu.VMEM((2, 4, 32, D), BF16),
            pltpu.VMEM((2, 4, 16, BLK), BF16),
            pltpu.VMEM((2, 4, 32, D), BF16),
            pltpu.VMEM((2, 4, 16, BLK), BF16),
            dma((5,)),
            dma((3 + 2 * NG,)),
            dma((3 + 2 * NG,)),
            dma((2,)),
            dma((2,)),
            dma((2, NG + 1, 3)),
            dma((2, NG + 1, 3)),
            dma((2, NG + 1)),
            dma((2, NG + 1)),
            dma((2, NG + 1)),
            dma((2, NG + 1)),
            dma((2, NG + 1, 4)),
            dma((2, NG + 1, 4)),
        ],
        compiler_params=pltpu.CompilerParams(
            collective_id=0, has_side_effects=True, vmem_limit_bytes=48 * 2**20
        ),
        name="routed_experts",
    )(fi, fr, fw, bg, br, bw, saved, gate, up, down)


def solution(mesh):
    placed = (
        P("pipe", "expert", None),
        P("pipe", "expert", None),
        P("pipe", "expert"),
        P("pipe", "expert", None),
        P("pipe", "expert", None),
        P("pipe", "expert"),
        P("pipe", None, None, None, "expert"),
        P("pipe", None, "expert"),
        P("pipe", None, "expert"),
        P("pipe", "expert", None),
    )
    return jax.shard_map(
        per_device,
        mesh=mesh,
        in_specs=placed,
        out_specs=(P("pipe", "expert", None), P("pipe", "expert", None)),
        check_vma=False,
    )
```

time: 526 us -> 124 us (0.24)
  waiting for transfers between devices: 297 us -> 0 us
  starting transfers between devices: 165 us -> 0 us
  Pallas kernels: 0 us -> 113 us
  local copies, waits for them, and re-layouts: 29.9 us -> 8.68 us
  matrix products: 20.6 us -> 0 us
  other arithmetic: 11.1 us -> 0 us
    all_to_all x4 -> x0, waiting for transfers between devices: 218 us -> none  [move_rows(): lax.all_to_all(blocks, 'expert', split_axis=0, concat_axis=0, tiled=True)]
    ppermute x2 -> x0, starting transfers between devices: 116 us -> none  [passed_along(): return lax.ppermute(block, axis, route)]
    pallas_call x0 -> x1, Pallas kernels: none -> 113 us  [per_device(): pl.pallas_call(kernel, out_shape=(rows_out, rows_out), in_specs=[vmem] *...]
    ppermute x2 -> x0, waiting for transfers between devices: 79.1 us -> none  [passed_along(): return lax.ppermute(block, axis, route)]
    all_to_all x4 -> x0, starting transfers between devices: 49.7 us -> none  [move_rows(): lax.all_to_all(blocks, 'expert', split_axis=0, concat_axis=0, tiled=True)]
    reshape x8 -> x0, local copies, waits for them, and re-layouts: 21.2 us -> none  [the longest x1 5.22 us: per_device(): received_bwd.reshape(rows_total, features)]
    dot_general x7 -> x0, matrix products: 20.6 us -> none  [the longest x1 8.15 us: expert_forward(): jnp.dot(hidden, down_local, preferred_element_type=jnp.float32)]
    unnamed x18 -> x21, local copies, waits for them, and re-layouts: 1.58 us -> 8.68 us
  transfers between devices with their start and end apart: 6 -> 0, of which waited for: 5 -> 0; matrix products, arithmetic and copies ran while one was open for 10% -> 0% of each run, Pallas kernels for 0% -> 0%
where the time goes in v1:
time: 124 us; the launch traced here: 122 us
  Pallas kernels  113 us (91%)
  local copies, waits for them, and re-layouts  8.68 us (7%)
    pallas_call x1, Pallas kernels, per_device(): pl.pallas_call(kernel, out_shape=(rows_out, rows_out), in_specs=[vmem] *...  113 us
    unnamed x21, local copies, waits for them, and re-layouts  8.68 us

profile of v1, /device:TPU:4, one launch (start us, length us, event | category | flops | bytes accessed | tf_op | source)
XLA Modules:
  0.0 122.1 jit_solution(5469626345947644385)
XLA Ops:
  0.6 0.0 copy-start.7
  0.6 0.0 copy-start.3
  0.6 0.8 copy.13.fr
  1.4 0.0 copy-done.7
  1.5 0.1 copy.14.br
  1.5 1.0 copy.12
  2.6 0.0 copy-start.5
  2.6 0.0 copy-start.6
  2.6 0.0 copy-done.3
  2.6 0.6 copy-done.5
  3.2 0.0 copy-done.6
  3.3 0.0 copy-start
  3.3 1.2 copy-done
  4.4 0.0 copy-start.1
  4.4 1.2 copy-done.1
  5.6 0.0 copy-start.2
  5.6 1.2 copy-done.2
  6.8 0.0 copy-start.4
  6.8 1.0 copy-done.4
  7.8 112.7 %routed_experts.1 = (bf16[1,64,3584]{2,1,0:T(8,128)(2,1)S(1)}, bf16[1,64,3584]{2,1,0:T(8,128)(2,1)S(1)}) custom-call(bf16[1,64,3584]{2,1,0:T(8,128)(2,1)S(1)} %copy-done.3, s32[1,64,1]{2,1,0:T(8,128)S(1)} %copy.13.fr, f32[1,64]{1,0:T(1,128)S(1)} %copy-done.5, bf16[1,64,3584]{2,1,0:T(8,128)(2,1)S(1)} %copy-done.4, s32[1,64,1]{2,1,0:T(8,128)S(1)} %copy.14.br, ...), custom_call_target="tpu_custom_call" | custom-call | tf_op jit(solution)/shard_map/routed_experts/pallas_call | solution.py:352
  120.6 0.8 copy.17
  121.3 0.8 copy.18
Async XLA Ops:
  0.6 0.8 copy-start.7
  0.6 2.0 %copy-start.3 = (bf16[1,64,3584]{2,1,0:T(8,128)(2,1)S(1)}, bf16[1,64,3584]{2,1,0:T(8,128)(2,1)}, u32[]{:S(2)}) copy-start(bf16[1,64,3584]{2,1,0:T(8,128)(2,1)} %fi.1) | copy-start | bytes 1376260
  2.6 0.7 copy-start.5
  2.6 0.7 copy-start.6
  3.3 1.2 copy-start
  4.4 1.2 copy-start.1
  5.6 1.2 copy-start.2
  6.8 1.0 copy-start.4

commit v2 on v1

--- a/solution.py
+++ b/solution.py
@@ -17,6 +17,8 @@
 GROUPS = ((0, 2), (2, 4), (4, 6), (6, 7))
 NG = len(GROUPS)
 FWD, BWD = 0, 1
+Z_LAG = 2
+W_AHEAD = 4
 
 
 def iota(shape, dim):
@@ -40,8 +42,13 @@
     return pl.ds(c * BLK, BLK)
 
 
+def column(values):
+    diagonal = iota((TOK, TOK), 0) == iota((TOK, TOK), 1)
+    spread = jnp.where(diagonal, jnp.broadcast_to(values.astype(F32), (TOK, TOK)), 0.0)
+    return jnp.broadcast_to(jnp.sum(spread, axis=1, keepdims=True), (TOK, 128))
+
+
 def row_index(route):
-    route = jnp.broadcast_to(route, (TOK, 128))
     to_one = (route == 1).astype(F32)
     earlier = (iota((TOK, TOK), 1) < iota((TOK, TOK), 0)).astype(BF16)
     ones_before = dot(earlier, to_one.astype(BF16))
@@ -66,9 +73,10 @@
 
 
 def kernel(
-    fi, fr, fw, bg, br, bw, saved, gate, up, down,
+    fi_in, fr_in, fw_in, bg_in, br_in, bw_in, saved, gate, up, down,
     out_f, out_b,
-    gw, uw, dw, sv,
+    fi, fr, fw, bg, br, bw,
+    gw, uw, dw, sv, sv_rows,
     ds_main, ds_extra, tok, tok_extra,
     info_s, info_r,
     acc_a, acc_b, act_a, act_b,
@@ -86,7 +94,6 @@
     turn = 1 - 2 * ((x + p) % 2)
     x_w = (x + turn + 4) % 4
     x_t = (x - turn + 4) % 4
-    x_far = (x + 2) % 4
     weight_peer = (p, z * 4 + x_w)
     token_peer = (p, z * 4 + x_t)
     after, before = (p + 1) % 16, (p + 15) % 16
@@ -109,73 +116,65 @@
         sends.append(copy)
         return copy
 
+    small = [
+        pltpu.make_async_copy(src, dst, loc_sem.at[4 + i])
+        for i, (src, dst) in enumerate(
+            ((br_in, br), (bw_in, bw), (bg_in, bg), (fr_in, fr), (fw_in, fw), (fi_in, fi))
+        )
+    ]
+    for copy in small:
+        copy.start()
     local = [
         pltpu.make_async_copy(gate.at[0], gw.at[:, pl.ds(0, UNITS)], loc_sem.at[0]),
         pltpu.make_async_copy(up.at[0], uw.at[:, pl.ds(0, UNITS)], loc_sem.at[1]),
         pltpu.make_async_copy(down.at[0], dw.at[pl.ds(0, UNITS)], loc_sem.at[2]),
-        pltpu.make_async_copy(saved.at[:, :, x], sv.at[0, 0], loc_sem.at[3]),
-        pltpu.make_async_copy(saved.at[:, :, x_t], sv.at[0, 1], loc_sem.at[4]),
+        pltpu.make_async_copy(saved, sv.at[0], loc_sem.at[3]),
     ]
     for copy in local:
         copy.start()
 
-    index_f = row_index(fr[0])
-    index_b = row_index(br[0])
-    info_s[BWD] = index_b
-    weight_spread = jnp.where(
-        iota((TOK, TOK), 0) == iota((TOK, TOK), 1), jnp.broadcast_to(fw[...], (TOK, TOK)), 0.0
-    )
-    weight_col = jnp.sum(weight_spread, axis=1, keepdims=True)
-    info_s[FWD] = jnp.where(
-        iota((TOK, 128), 1) == 1, jnp.broadcast_to(weight_col, (TOK, 128)), index_f
-    )
-    grad_spread = jnp.where(
-        iota((TOK, TOK), 0) == iota((TOK, TOK), 1), jnp.broadcast_to(bw[...], (TOK, TOK)), 0.0
-    )
-    grad_col = jnp.sum(grad_spread, axis=1, keepdims=True)
-
-    def pick(mb, index, read):
-        by_lane = tokens_in_lanes(index)
+    def read_grad(c):
+        return (grad_col[:, :1] * bg[0, :, block_cols(c)].astype(F32)).astype(BF16)
+
+    def read_input(c):
+        return fi[0, :, block_cols(c)]
+
+    def pick_main(mb, by_lane, read, g):
         row = iota((TOK, TOK), 0)
         picker = (by_lane == ((row >> 5) * CAP + (row & 31)).astype(F32)).astype(BF16)
+        for c in range(*GROUPS[g]):
+            picked = dot(picker, read(c)).astype(BF16)
+            ds_main[mb, 0, :, block_cols(c)] = picked[:32]
+            ds_main[mb, 1, :, block_cols(c)] = picked[32:]
+        tok[mb, 0, z, :, group_cols(g)] = ds_main[mb, z // 2, :, group_cols(g)]
+
+    def pick_extra(mb, by_lane, read):
         row = iota((32, TOK), 0)
         extra_id = (row >> 4) * CAP + 32 + (row & 1)
         extra = jnp.zeros((32, BLK), F32)
         for c in range(NBLK):
-            values = read(c)
-            picked = dot(picker, values).astype(BF16)
-            ds_main[mb, 0, :, block_cols(c)] = picked[:32]
-            ds_main[mb, 1, :, block_cols(c)] = picked[32:]
             wanted = jnp.where(((row & 15) >> 1) == c, extra_id, -1).astype(F32)
-            extra += dot((by_lane[:32] == wanted).astype(BF16), values)
+            extra += dot((by_lane[:32] == wanted).astype(BF16), read(c))
         extra = extra.astype(BF16)
         ds_extra[mb, 0] = extra[:16]
         ds_extra[mb, 1] = extra[16:]
-        tok[mb, 0, z] = ds_main[mb, z // 2]
         tok_extra[mb, 0, z] = ds_extra[mb, z // 2]
-
-    def read_grad(c):
-        return (grad_col * bg[0, :, block_cols(c)].astype(F32)).astype(BF16)
-
-    def read_input(c):
-        return fi[0, :, block_cols(c)]
 
     zd = {}
     xd = {}
 
-    def send_rows(mb):
-        for g in (NG, *range(NG)):
-            for dz in (2, 1, 3):
-                tz = (z + dz) % 4
-                if g == NG:
-                    src, dst = ds_extra.at[mb, tz // 2], tok_extra.at[mb, 0, z]
-                else:
-                    src = ds_main.at[mb, tz // 2, :, group_cols(g)]
-                    dst = tok.at[mb, 0, z, :, group_cols(g)]
-                zd[mb, g, dz] = remote(
-                    src, dst, zd_send.at[mb, g, dz - 1], zd_recv.at[mb, g, dz - 1],
-                    (p, tz * 4 + x),
-                )
+    def send_rows(mb, g):
+        for dz in (2, 1, 3):
+            tz = (z + dz) % 4
+            if g == NG:
+                src, dst = ds_extra.at[mb, tz // 2], tok_extra.at[mb, 0, z]
+            else:
+                src = ds_main.at[mb, tz // 2, :, group_cols(g)]
+                dst = tok.at[mb, 0, z, :, group_cols(g)]
+            zd[mb, g, dz] = remote(
+                src, dst, zd_send.at[mb, g, dz - 1], zd_recv.at[mb, g, dz - 1],
+                (p, tz * 4 + x),
+            )
 
     def pass_rows(mb, g):
         for dz in range(1, 4):
@@ -187,32 +186,58 @@
             dst = tok.at[mb, 1, :, :, group_cols(g)]
         xd[mb, g] = remote(src, dst, xd_send.at[mb, g], xd_recv.at[mb, g], token_peer)
 
-    pick(BWD, index_b, read_grad)
+    from_gate, from_up = [], []
+
+    def send_weights(g):
+        cols = group_cols(g)
+        from_gate.append(remote(
+            gate.at[0, cols], gw.at[cols, pl.ds(UNITS, UNITS)],
+            w_send.at[2 + g], w_recv.at[2 + g], weight_peer))
+        from_up.append(remote(
+            up.at[0, cols], uw.at[cols, pl.ds(UNITS, UNITS)],
+            w_send.at[2 + NG + g], w_recv.at[2 + NG + g], weight_peer))
+
+    for copy in small[:3]:
+        copy.wait()
+    index_b = row_index(column(br[...]))
+    grad_col = column(bw[...])
+    info_s[BWD] = index_b
+    lanes_b = tokens_in_lanes(index_b)
     pl.semaphore_wait(barrier, len(peers))
 
     from_down = remote(down.at[0], dw.at[pl.ds(UNITS, UNITS)], w_send.at[0], w_recv.at[0], weight_peer)
-    from_saved = [
-        remote(saved.at[:, :, x_w], sv.at[1, 0], w_send.at[1], w_recv.at[1], weight_peer),
-        remote(saved.at[:, :, x_far], sv.at[1, 1], w_send.at[2], w_recv.at[2], weight_peer),
-    ]
-    send_rows(BWD)
+    from_saved = remote(saved, sv.at[1], w_send.at[1], w_recv.at[1], weight_peer)
+    for g in range(NG):
+        pick_main(BWD, lanes_b, read_grad, g)
+        send_rows(BWD, g)
+    pick_extra(BWD, lanes_b, read_grad)
+    send_rows(BWD, NG)
+
+    for copy in small[3:]:
+        copy.wait()
+    index_f = row_index(column(fr[...]))
+    info_s[FWD] = jnp.where(iota((TOK, 128), 1) == 1, column(fw[...]), index_f)
+    lanes_f = tokens_in_lanes(index_f)
     infos = [
         remote(info_s.at[FWD], info_r.at[FWD], i_send.at[FWD], i_recv.at[FWD], (after, e)),
         remote(info_s.at[BWD], info_r.at[BWD], i_send.at[BWD], i_recv.at[BWD], (before, e)),
     ]
-    pick(FWD, index_f, read_input)
-    send_rows(FWD)
-
-    for g in (NG, *range(NG)):
+    pick_extra(FWD, lanes_f, read_input)
+    for g in range(NG):
+        pick_main(FWD, lanes_f, read_input, g)
+
+    forward_order = [NG, *range(NG)]
+    for g in range(NG):
         pass_rows(BWD, g)
-
-    from_gate, from_up = [], []
-    for g in range(NG):
-        cols = group_cols(g)
-        from_gate.append(remote(
-            gate.at[0, cols], gw.at[cols, pl.ds(UNITS, UNITS)], w_send.at[3 + g], w_recv.at[3 + g], weight_peer))
-        from_up.append(remote(
-            up.at[0, cols], uw.at[cols, pl.ds(UNITS, UNITS)], w_send.at[3 + NG + g], w_recv.at[3 + NG + g], weight_peer))
+        if g >= Z_LAG:
+            send_rows(FWD, forward_order[g - Z_LAG])
+        if g == NG - 2:
+            send_weights(0)
+    pass_rows(BWD, NG)
+    for g in forward_order[max(NG - Z_LAG, 0):]:
+        send_rows(FWD, g)
+    for g in range(1, W_AHEAD):
+        send_weights(g)
 
     def rows_of(mb, c):
         main = tok[mb, :, :, :, block_cols(c)].reshape(256, BLK)
@@ -228,17 +253,20 @@
         xd[BWD, g].wait_recv()
         for c in range(*GROUPS[g]):
             acc_a[...] += dot_t(rows_of(BWD, c), dw[:, block_cols(c)])
-    for copy in from_saved:
-        copy.wait_recv()
-
-    def saved_rows(kind, h):
-        main = sv[h, :, kind, :, 0:32, :].reshape(256, UNITS).astype(F32)
-        extra = [sv[h, w, kind, s, 32:34, :].astype(F32) for w in range(2) for s in range(4)]
-        return jnp.concatenate([main, *extra], axis=0)
+    from_saved.wait_recv()
+    row, col = iota((272, 544), 0), iota((272, 544), 1)
+    late = row >= 256
+    source = jnp.where(late, (row - 256) >> 1, row >> 5)
+    slot = jnp.where(late, 32 + (row & 1), row & 31)
+    holder = (source & 3) * 4 + jnp.where(source >= 4, x_t, x)
+    chooser = (((col >> 4) == slot) & ((col & 15) == holder)).astype(BF16)
+    for h in range(2):
+        for kind in range(2):
+            sv_rows[kind, :, h * UNITS:(h + 1) * UNITS] = dot(chooser, sv[h, kind].reshape(544, UNITS))
 
     for h in range(2):
         lanes = pl.ds(h * UNITS, UNITS)
-        g_pre, u_pre = saved_rows(0, h), saved_rows(1, h)
+        g_pre, u_pre = sv_rows[0, :, lanes], sv_rows[1, :, lanes]
         sig = jax.nn.sigmoid(g_pre)
         grad = acc_a[:, lanes]
         act_a[:, lanes] = (grad * u_pre * sig * (1.0 + g_pre * (1.0 - sig))).astype(BF16)
@@ -280,15 +308,18 @@
                 src, dst, zc_send.at[mb, g, dz], zc_recv.at[mb, g, dz], (section, tz * 4 + x))
 
     own_extra[...] = jnp.zeros_like(own_extra)
-    pass_rows(FWD, NG)
-    for g in range(NG):
-        pass_rows(FWD, g)
+    for g in range(NG):
         from_gate[g].wait_recv()
         from_up[g].wait_recv()
         for c in range(*GROUPS[g]):
             rows = block_cols(c)
             keep(BWD, c, dot_t(act_a[...], gw[rows]) + dot_t(act_b[...], uw[rows]))
+        if g + W_AHEAD < NG:
+            send_weights(g + W_AHEAD)
         send_part(BWD, g)
+        if g == 0:
+            pass_rows(FWD, NG)
+        pass_rows(FWD, g)
         if g > 0:
             send_sum(BWD, g - 1)
     send_part(BWD, NG)
@@ -345,20 +376,28 @@
 
 def per_device(fi, fr, fw, bg, br, bw, saved, gate, up, down):
     vmem = pl.BlockSpec(memory_space=pltpu.VMEM)
-    anywhere = pl.BlockSpec(memory_space=pl.ANY)
+    hbm = pl.BlockSpec(memory_space=pltpu.HBM)
     dma = pltpu.SemaphoreType.DMA
     rows_out = jax.ShapeDtypeStruct((1, TOK, D), BF16)
-    saved = saved[0].reshape(2, 4, 4, CAP, UNITS)
+    saved = saved[0].transpose(0, 2, 1, 3)
+    fr, br = fr.reshape(1, TOK), br.reshape(1, TOK)
     return pl.pallas_call(
         kernel,
         out_shape=(rows_out, rows_out),
-        in_specs=[vmem] * 6 + [anywhere] * 4,
+        in_specs=[hbm] * 10,
         out_specs=(vmem, vmem),
         scratch_shapes=[
+            pltpu.VMEM((1, TOK, D), BF16),
+            pltpu.VMEM((1, TOK), jnp.int32),
+            pltpu.VMEM((1, TOK), F32),
+            pltpu.VMEM((1, TOK, D), BF16),
+            pltpu.VMEM((1, TOK), jnp.int32),
+            pltpu.VMEM((1, TOK), F32),
             pltpu.VMEM((D, 2 * UNITS), BF16),
             pltpu.VMEM((D, 2 * UNITS), BF16),
             pltpu.VMEM((2 * UNITS, D), BF16),
-            pltpu.VMEM((2, 2, 2, 4, CAP, UNITS), BF16),
+            pltpu.VMEM((2, 2, CAP, 16, UNITS), BF16),
+            pltpu.VMEM((2, 272, 256), F32),
             pltpu.VMEM((2, 2, 32, D), BF16),
             pltpu.VMEM((2, 2, 16, BLK), BF16),
             pltpu.VMEM((2, 2, 4, 32, D), BF16),
@@ -379,9 +418,9 @@
             pltpu.VMEM((2, 4, 16, BLK), BF16),
             pltpu.VMEM((2, 4, 32, D), BF16),
             pltpu.VMEM((2, 4, 16, BLK), BF16),
-            dma((5,)),
-            dma((3 + 2 * NG,)),
-            dma((3 + 2 * NG,)),
+            dma((10,)),
+            dma((2 + 2 * NG,)),
+            dma((2 + 2 * NG,)),
             dma((2,)),
             dma((2,)),
             dma((2, NG + 1, 3)),
@@ -394,7 +433,7 @@
             dma((2, NG + 1, 4)),
         ],
         compiler_params=pltpu.CompilerParams(
-            collective_id=0, has_side_effects=True, vmem_limit_bytes=48 * 2**20
+            collective_id=0, has_side_effects=True, vmem_limit_bytes=60 * 2**20
         ),
         name="routed_experts",
     )(fi, fr, fw, bg, br, bw, saved, gate, up, down)

time: 124 us -> 115 us (0.927); the launches traced: 122 us -> 115 us
  local copies, waits for them, and re-layouts: 8.68 us -> 2.64 us
  Pallas kernels: 113 us -> 111 us
    unnamed x21 -> x4, local copies, waits for them, and re-layouts: 8.68 us -> 2.64 us
    pallas_call x1, Pallas kernels: 113 us -> 111 us  [per_device(): pl.pallas_call(kernel, out_shape=(rows_out, rows_out), in_specs=[hbm] * 1...]
where the time goes in v2:
time: 115 us
  Pallas kernels  111 us (97%)
  local copies, waits for them, and re-layouts  2.64 us (2%)
    pallas_call x1, Pallas kernels, per_device(): pl.pallas_call(kernel, out_shape=(rows_out, rows_out), in_specs=[hbm] * 1...  111 us
    unnamed x4, local copies, waits for them, and re-layouts  2.64 us

profile of v2, /device:TPU:4, one launch (start us, length us, event | category | flops | bytes accessed | tf_op | source)
XLA Modules:
  0.0 114.6 jit_solution(12563721878661178260)
XLA Ops:
  0.6 111.3 %routed_experts.1 = (bf16[1,64,3584]{2,1,0:T(8,128)(2,1)}, bf16[1,64,3584]{2,1,0:T(8,128)(2,1)}) custom-call(bf16[1,64,3584]{2,1,0:T(8,128)(2,1)} %fi_in.1, s32[1,64]{1,0:T(1,128)} %bitcast.6, f32[1,64]{1,0:T(1,128)} %fw_in.1, bf16[1,64,3584]{2,1,0:T(8,128)(2,1)} %bg_in.1, s32[1,64]{1,0:T(1,128)} %bitcast.7, f32[1,64]{1,0:T(1,128)} %bw_in.1, ...), custom_call_target="tpu_custom_call" | custom-call | tf_op jit(solution)/shard_map/routed_experts/pallas_call | solution.py:384
  111.9 0.0 copy-start
  111.9 1.9 %copy.14 = bf16[1,64,3584]{2,1,0:T(8,128)(2,1)} copy(bf16[1,64,3584]{2,1,0:T(8,128)(2,1)} %get-tuple-element.4) | data formatting | bytes 917504
  113.8 0.0 copy-done
  113.8 0.8 copy.15
Async XLA Ops:
  111.9 1.9 %copy-start = (bf16[1,64,3584]{2,1,0:T(8,128)(2,1)S(1)}, bf16[1,64,3584]{2,1,0:T(8,128)(2,1)}, u32[]{:S(2)}) copy-start(bf16[1,64,3584]{2,1,0:T(8,128)(2,1)} %get-tuple-element.5) | copy-start | bytes 1376260

commit v3 on v2

v3 whole, which is shorter than its diff:
```python
import jax
import jax.numpy as jnp
from jax import lax
from jax.experimental import pallas as pl
from jax.experimental.pallas import tpu as pltpu
from jax.sharding import PartitionSpec as P

MESH = pl.DeviceIdType.MESH
BF16 = jnp.bfloat16
F32 = jnp.float32
CAP = 34
TOK = 64
D = 3584
UNITS = 128
BLK = 512
NBLK = D // BLK
HALF = BLK // 2
WIDE = D + HALF
TAIL = pl.ds(D, HALF)
GROUPS = ((0, 2), (2, 4), (4, 6), (6, 7))
NG = len(GROUPS)
FWD, BWD = 0, 1
STEPS = (0, 2, 1, 3)
W_FIRST = 2
W_AHEAD = 4
B_LAG = 2
F_OWN_EARLY = True


def iota(shape, dim):
    return lax.broadcasted_iota(jnp.int32, shape, dim)


def dot(a, b):
    return jnp.dot(a, b, preferred_element_type=F32)


def dot_t(a, b):
    return lax.dot_general(a, b, (((1,), (1,)), ((), ())), preferred_element_type=F32)


def group_cols(g):
    first, last = GROUPS[g]
    return pl.ds(first * BLK, (last - first) * BLK)


def message_cols(g):
    first, last = GROUPS[g]
    return pl.ds(first * BLK, (last - first) * BLK + (HALF if g == NG - 1 else 0))


def block_cols(c):
    return pl.ds(c * BLK, BLK)


def column(values):
    diagonal = iota((TOK, TOK), 0) == iota((TOK, TOK), 1)
    spread = jnp.where(diagonal, jnp.broadcast_to(values.astype(F32), (TOK, TOK)), 0.0)
    return jnp.broadcast_to(jnp.sum(spread, axis=1, keepdims=True), (TOK, 128))


def row_index(route):
    to_one = (route == 1).astype(F32)
    earlier = (iota((TOK, TOK), 1) < iota((TOK, TOK), 0)).astype(BF16)
    ones_before = dot(earlier, to_one.astype(BF16))
    place = iota((TOK, 128), 0).astype(F32)
    return jnp.where(route == 1, CAP + ones_before, place - ones_before)


def tokens_in_lanes(index):
    diagonal = iota((TOK, TOK), 0) == iota((TOK, TOK), 1)
    spread = jnp.where(diagonal, index[:, :TOK], 0.0).astype(BF16)
    return dot(jnp.ones((TOK, TOK), BF16), spread)


def extra_match(short, long, c, half):
    if half is None:
        source = short >> 1
    else:
        source = jnp.where(short < 8, ((short >> 2) << 2) + 2 * half + ((short >> 1) & 1), -1)
    return (((long >> 4) == source) & ((long & 15) == 2 * c + (short & 1))).astype(BF16)


def unpack_extra(c, packed):
    short, long = iota((16, packed.shape[0]), 0), iota((16, packed.shape[0]), 1)
    source = short >> 1
    place = 2 * c + (short & 1)
    parts = [
        dot((((long >> 5) == source) & ((long & 31) == place + up)).astype(BF16), packed)
        for up in (0, 16)
    ]
    return jnp.concatenate(parts, axis=1).astype(BF16)


def pack_extra(c, half):
    return extra_match(iota((128, 16), 1), iota((128, 16), 0), c, half)


def kernel(
    fi_in, fr_in, fw_in, bg_in, br_in, bw_in, saved, gate, up, down,
    out_f, out_b,
    fi, fr, fw, bg, br, bw,
    gw, uw, dw, sv, sv_rows, sv_send,
    ds_main, tok,
    info_s, info_r,
    acc_a, acc_b, act_a, act_b,
    own, own_extra,
    xs, xr, zs, zr,
    loc_sem,
    w_send, w_recv, i_send, i_recv,
    zd_send, zd_recv, xd_send, xd_recv,
    xc_send, xc_recv, zc_send, zc_recv,
):
    p = lax.axis_index("pipe")
    e = lax.axis_index("expert")
    z, x = e // 4, e % 4
    turn = 1 - 2 * ((x + p) % 2)
    x_w = (x + turn + 4) % 4
    x_t = (x - turn + 4) % 4
    weight_peer = (p, z * 4 + x_w)
    token_peer = (p, z * 4 + x_t)
    after, before = (p + 1) % 16, (p + 15) % 16

    barrier = pltpu.get_barrier_semaphore()
    peers = [weight_peer, token_peer]
    peers += [(p, ((z + dz) % 4) * 4 + x) for dz in range(1, 4)]
    peers += [(q, ((z + dz) % 4) * 4 + x) for q in (after, before) for dz in range(4)]
    for peer in peers:
        pl.semaphore_signal(barrier, inc=1, device_id=peer, device_id_type=MESH)

    sends = []

    def remote(src, dst, send, recv, peer):
        copy = pltpu.make_async_remote_copy(
            src_ref=src, dst_ref=dst, send_sem=send, recv_sem=recv,
            device_id=peer, device_id_type=MESH,
        )
        copy.start()
        sends.append(copy)
        return copy

    small = [
        pltpu.make_async_copy(src, dst, loc_sem.at[4 + i])
        for i, (src, dst) in enumerate(
            ((br_in, br), (bw_in, bw), (bg_in, bg), (fr_in, fr), (fw_in, fw), (fi_in, fi))
        )
    ]
    for copy in small:
        copy.start()
    local = [
        pltpu.make_async_copy(gate.at[0], gw.at[:, pl.ds(0, UNITS)], loc_sem.at[0]),
        pltpu.make_async_copy(up.at[0], uw.at[:, pl.ds(0, UNITS)], loc_sem.at[1]),
        pltpu.make_async_copy(down.at[0], dw.at[pl.ds(0, UNITS)], loc_sem.at[2]),
        pltpu.make_async_copy(saved, sv, loc_sem.at[3]),
    ]
    for copy in local:
        copy.start()

    def read_grad(c):
        return (grad_col[:, :1] * bg[0, :, block_cols(c)].astype(F32)).astype(BF16)

    def read_input(c):
        return fi[0, :, block_cols(c)]

    def pick_main(mb, by_lane, read, g):
        row = iota((TOK, TOK), 0)
        picker = (by_lane == ((row >> 5) * CAP + (row & 31)).astype(F32)).astype(BF16)
        for c in range(*GROUPS[g]):
            picked = dot(picker, read(c)).astype(BF16)
            ds_main[mb, 0, :, block_cols(c)] = picked[:32]
            ds_main[mb, 1, :, block_cols(c)] = picked[32:]

    def pick_extra(mb, by_lane, read):
        row = iota((32, TOK), 0)
        extra_id = (row >> 4) * CAP + 32 + (row & 1)
        extra = jnp.zeros((32, BLK), F32)
        for c in range(NBLK):
            wanted = jnp.where(((row & 15) >> 1) == c, extra_id, -1).astype(F32)
            extra += dot((by_lane[:32] == wanted).astype(BF16), read(c))
        extra = extra.astype(BF16)
        for k in range(2):
            ds_main[mb, k, 0:16, TAIL] = extra[16 * k:16 * k + 16, :HALF]
            ds_main[mb, k, 16:32, TAIL] = extra[16 * k:16 * k + 16, HALF:]
        tok[mb, 0, 0] = ds_main[mb, z // 2]

    zd = {}
    xd = {}

    def send_rows(mb, at):
        tz = (z + STEPS[at]) % 4
        zd[mb, at] = remote(
            ds_main.at[mb, tz // 2], tok.at[mb, 0, at],
            zd_send.at[mb, at - 1], zd_recv.at[mb, at - 1], (p, tz * 4 + x))

    def pass_rows(mb, at):
        if at > 0:
            zd[mb, at].wait_recv()
        xd[mb, at] = remote(
            tok.at[mb, 0, at], tok.at[mb, 1, at], xd_send.at[mb, at], xd_recv.at[mb, at], token_peer)

    def wait_rows(mb, at):
        xd[mb, at].wait_recv()

    from_gate, from_up = [], []

    def send_weights(g):
        cols = group_cols(g)
        from_gate.append(remote(
            gate.at[0, cols], gw.at[cols, pl.ds(UNITS, UNITS)],
            w_send.at[2 + g], w_recv.at[2 + g], weight_peer))
        from_up.append(remote(
            up.at[0, cols], uw.at[cols, pl.ds(UNITS, UNITS)],
            w_send.at[2 + NG + g], w_recv.at[2 + NG + g], weight_peer))

    pl.semaphore_wait(barrier, len(peers))
    from_down = remote(down.at[0], dw.at[pl.ds(UNITS, UNITS)], w_send.at[0], w_recv.at[0], weight_peer)
    for copy in small[:3]:
        copy.wait()
    index_b = row_index(column(br[...]))
    grad_col = column(bw[...])
    info_s[BWD] = index_b
    lanes_b = tokens_in_lanes(index_b)
    for g in range(NG):
        pick_main(BWD, lanes_b, read_grad, g)
    pick_extra(BWD, lanes_b, read_grad)
    for at in range(1, 4):
        send_rows(BWD, at)
    pass_rows(BWD, 0)

    for copy in local:
        copy.wait()
    row, col = iota((272, 544), 0), iota((272, 544), 1)
    late = row >= 256
    source = jnp.where(late, (row - 256) >> 1, row >> 5)
    slot = jnp.where(late, 32 + (row & 1), row & 31)
    step = ((source & 1) << 1) | ((source >> 1) & 1)
    holder = ((z + 4 - step) & 3) * 4
    in_slot = (col >> 4) == slot
    mine = holder + jnp.where(source >= 4, x_t, x) == (col & 15)
    theirs = holder + jnp.where(source >= 4, (x + 2) % 4, x_w) == (col & 15)
    for kind in range(2):
        stored = sv[kind].reshape(544, UNITS)
        sv_send[kind] = dot((in_slot & theirs).astype(BF16), stored).astype(BF16)
        sv_rows[kind, :, 0:UNITS] = dot((in_slot & mine).astype(BF16), stored).astype(BF16)
    from_saved = remote(
        sv_send, sv_rows.at[:, :, pl.ds(UNITS, UNITS)], w_send.at[1], w_recv.at[1], weight_peer)

    for copy in small[3:]:
        copy.wait()
    index_f = row_index(column(fr[...]))
    info_s[FWD] = jnp.where(iota((TOK, 128), 1) == 1, column(fw[...]), index_f)
    lanes_f = tokens_in_lanes(index_f)
    infos = [
        remote(info_s.at[FWD], info_r.at[FWD], i_send.at[FWD], i_recv.at[FWD], (after, e)),
        remote(info_s.at[BWD], info_r.at[BWD], i_send.at[BWD], i_recv.at[BWD], (before, e)),
    ]
    for g in range(NG):
        pick_main(FWD, lanes_f, read_input, g)
    pick_extra(FWD, lanes_f, read_input)

    for g in range(W_FIRST):
        send_weights(g)
    if F_OWN_EARLY:
        pass_rows(FWD, 0)
    pass_rows(BWD, 2)
    send_rows(FWD, 1)
    pass_rows(BWD, 3)
    send_rows(FWD, 2)
    send_rows(FWD, 3)
    pass_rows(BWD, 1)
    for g in range(W_FIRST, W_AHEAD):
        send_weights(g)

    def rows_of(mb, c, half):
        count = 4 if half is None else 2
        first = 2 * half if half else 0
        main = tok[mb, :, first:first + count, :, block_cols(c)].reshape(64 * count, BLK)
        packed = tok[mb, :, first:first + count, :, TAIL].reshape(64 * count, HALF)
        extra = unpack_extra(c, packed)
        return jnp.concatenate([main, extra], axis=0)

    from_down.wait_recv()
    acc_a[...] = jnp.zeros_like(acc_a)
    for at in range(4):
        wait_rows(BWD, at)
    for c in range(NBLK):
        acc_a[...] += dot_t(rows_of(BWD, c, None), dw[:, block_cols(c)])
    from_saved.wait_recv()
    for h in range(2):
        lanes = pl.ds(h * UNITS, UNITS)
        g_pre, u_pre = sv_rows[0, :, lanes].astype(F32), sv_rows[1, :, lanes].astype(F32)
        sig = jax.nn.sigmoid(g_pre)
        grad = acc_a[:, lanes]
        act_a[:, lanes] = (grad * u_pre * sig * (1.0 + g_pre * (1.0 - sig))).astype(BF16)
        act_b[:, lanes] = (grad * g_pre * sig).astype(BF16)

    xc, zc = {}, {}

    def span(half):
        return (0, 4) if half is None else (2 * half, 2)

    def keep(mb, c, value, half):
        first, count = span(half)
        rows = 32 * count
        own[32 * first:32 * first + rows, block_cols(c)] = value[:rows]
        xs[mb, first:first + count, :, block_cols(c)] = (
            value[rows:2 * rows].astype(BF16).reshape(count, 32, BLK))
        own_extra[...] += dot(pack_extra(c, half), value[2 * rows:].astype(BF16))

    def send_part(mb, g, half):
        first, count = span(half)
        some = pl.ds(first, count)
        if g == NG - 1:
            packed = own_extra[64 + 16 * first:64 + 16 * (first + count)].astype(BF16).reshape(count, 16, BLK)
            xs[mb, first:first + count, 0:16, TAIL] = packed[:, :, :HALF]
            xs[mb, first:first + count, 16:32, TAIL] = packed[:, :, HALF:]
        src, dst = xs.at[mb, some, :, message_cols(g)], xr.at[mb, some, :, message_cols(g)]
        h = half or 0
        xc[mb, g, h] = remote(src, dst, xc_send.at[mb, h, g], xc_recv.at[mb, h, g], token_peer)

    def send_sum(mb, g, half):
        section = after if mb == FWD else before
        first, count = span(half)
        xc[mb, g, half or 0].wait_recv()
        if g == NG - 1:
            packed = own_extra[16 * first:16 * (first + count)].reshape(count, 16, BLK)
            for top, lanes in ((0, slice(0, HALF)), (16, slice(HALF, BLK))):
                zs[mb, first:first + count, top:top + 16, TAIL] = (
                    packed[:, :, lanes] + xr[mb, first:first + count, top:top + 16, TAIL].astype(F32)
                ).astype(BF16)
        for c in range(*GROUPS[g]):
            cols = block_cols(c)
            zs[mb, first:first + count, :, cols] = (
                own[32 * first:32 * (first + count), cols].reshape(count, 32, BLK)
                + xr[mb, first:first + count, :, cols].astype(F32)
            ).astype(BF16)
        for at in (1, 2, 3, 0):
            if not first <= at < first + count:
                continue
            tz = (z + 4 - STEPS[at]) % 4
            src, dst = zs.at[mb, at, :, message_cols(g)], zr.at[mb, at, :, message_cols(g)]
            zc[mb, g, at] = remote(
                src, dst, zc_send.at[mb, g, at], zc_recv.at[mb, g, at], (section, tz * 4 + x))

    own_extra[...] = jnp.zeros_like(own_extra)
    for g in range(NG):
        from_gate[g].wait_recv()
        from_up[g].wait_recv()
        for c in range(*GROUPS[g]):
            rows = block_cols(c)
            keep(BWD, c, dot_t(act_a[...], gw[rows]) + dot_t(act_b[...], uw[rows]), None)
        if g + W_AHEAD < NG:
            send_weights(g + W_AHEAD)
        send_part(BWD, g, None)
        if g >= B_LAG:
            send_sum(BWD, g - B_LAG, None)
    if not F_OWN_EARLY:
        pass_rows(FWD, 0)
    pass_rows(FWD, 1)
    for g in range(max(NG - B_LAG, 0), NG):
        send_sum(BWD, g, None)
    pass_rows(FWD, 2)
    pass_rows(FWD, 3)

    for half in range(2):
        for at in (2 * half, 2 * half + 1):
            wait_rows(FWD, at)
        acc_a[:144] = jnp.zeros((144, 256), F32)
        acc_b[:144] = jnp.zeros((144, 256), F32)
        for c in range(NBLK):
            rows = rows_of(FWD, c, half)
            acc_a[:144] += dot(rows, gw[block_cols(c)])
            acc_b[:144] += dot(rows, uw[block_cols(c)])
        act_a[:144] = (jax.nn.silu(acc_a[:144]) * acc_b[:144]).astype(BF16)
        own_extra[...] = jnp.zeros_like(own_extra)
        for g in range(NG):
            for c in range(*GROUPS[g]):
                keep(FWD, c, dot(act_a[:144], dw[:, block_cols(c)]), half)
            send_part(FWD, g, half)
        for g in range(NG):
            send_sum(FWD, g, half)

    def place(mb, out):
        infos[mb].wait_recv()
        info = info_r[mb]
        index = info[:, 0:1]
        def first_row(at):
            step = ((at & 1) << 1) | (at >> 1)
            return (((z + step) & 3) >> 1) * CAP

        col = iota((TOK, 128), 1)
        whole = (index == (first_row(col >> 5) + (col & 31)).astype(F32)).astype(BF16)
        extra_id = first_row(col >> 5) + 32 + (col & 1)
        for g in range(NG):
            for at in range(4):
                zc[mb, g, at].wait_recv()
        packed = zr[mb, :, :, TAIL].reshape(128, HALF)
        for c in range(NBLK):
            value = dot(whole, zr[mb, :, :, block_cols(c)].reshape(128, BLK))
            extra = []
            for up in (0, 8):
                wanted = jnp.where(((col & 31) >> 1) == c + up, extra_id, -1).astype(F32)
                extra.append(dot((index == wanted).astype(BF16), packed))
            value += jnp.concatenate(extra, axis=1)
            if mb == FWD:
                value = info[:, 1:2] * value
            out[0, :, block_cols(c)] = value.astype(BF16)

    place(BWD, out_b)
    place(FWD, out_f)
    for copy in sends:
        copy.wait_send()


def per_device(fi, fr, fw, bg, br, bw, saved, gate, up, down):
    vmem = pl.BlockSpec(memory_space=pltpu.VMEM)
    hbm = pl.BlockSpec(memory_space=pltpu.HBM)
    dma = pltpu.SemaphoreType.DMA
    rows_out = jax.ShapeDtypeStruct((1, TOK, D), BF16)
    saved = saved[0].transpose(0, 2, 1, 3)
    fr, br = fr.reshape(1, TOK), br.reshape(1, TOK)
    return pl.pallas_call(
        kernel,
        out_shape=(rows_out, rows_out),
        in_specs=[hbm] * 10,
        out_specs=(vmem, vmem),
        scratch_shapes=[
            pltpu.VMEM((1, TOK, D), BF16),
            pltpu.VMEM((1, TOK), jnp.int32),
            pltpu.VMEM((1, TOK), F32),
            pltpu.VMEM((1, TOK, D), BF16),
            pltpu.VMEM((1, TOK), jnp.int32),
            pltpu.VMEM((1, TOK), F32),
            pltpu.VMEM((D, 2 * UNITS), BF16),
            pltpu.VMEM((D, 2 * UNITS), BF16),
            pltpu.VMEM((2 * UNITS, D), BF16),
            pltpu.VMEM((2, CAP, 16, UNITS), BF16),
            pltpu.VMEM((2, 272, 256), BF16),
            pltpu.VMEM((2, 272, UNITS), BF16),
            pltpu.VMEM((2, 2, 32, WIDE), BF16),
            pltpu.VMEM((2, 2, 4, 32, WIDE), BF16),
            pltpu.VMEM((2, TOK, 128), F32),
            pltpu.VMEM((2, TOK, 128), F32),
            pltpu.VMEM((272, 256), F32),
            pltpu.VMEM((272, 256), F32),
            pltpu.VMEM((272, 256), BF16),
            pltpu.VMEM((272, 256), BF16),
            pltpu.VMEM((128, D), F32),
            pltpu.VMEM((128, BLK), F32),
            pltpu.VMEM((2, 4, 32, WIDE), BF16),
            pltpu.VMEM((2, 4, 32, WIDE), BF16),
            pltpu.VMEM((2, 4, 32, WIDE), BF16),
            pltpu.VMEM((2, 4, 32, WIDE), BF16),
            dma((10,)),
            dma((2 + 2 * NG,)),
            dma((2 + 2 * NG,)),
            dma((2,)),
            dma((2,)),
            dma((2, 3)),
            dma((2, 3)),
            dma((2, 4)),
            dma((2, 4)),
            dma((2, 2, NG)),
            dma((2, 2, NG)),
            dma((2, NG, 4)),
            dma((2, NG, 4)),
        ],
        compiler_params=pltpu.CompilerParams(
            collective_id=0, has_side_effects=True, vmem_limit_bytes=60 * 2**20
        ),
        name="routed_experts",
    )(fi, fr, fw, bg, br, bw, saved, gate, up, down)


def solution(mesh):
    placed = (
        P("pipe", "expert", None),
        P("pipe", "expert", None),
        P("pipe", "expert"),
        P("pipe", "expert", None),
        P("pipe", "expert", None),
        P("pipe", "expert"),
        P("pipe", None, None, None, "expert"),
        P("pipe", None, "expert"),
        P("pipe", None, "expert"),
        P("pipe", "expert", None),
    )
    return jax.shard_map(
        per_device,
        mesh=mesh,
        in_specs=placed,
        out_specs=(P("pipe", "expert", None), P("pipe", "expert", None)),
        check_vma=False,
    )
```

time: 115 us -> 109 us (0.948)
  Pallas kernels: 111 us -> 105 us
    pallas_call x1, Pallas kernels: 111 us -> 105 us  [per_device(): pl.pallas_call(kernel, out_shape=(rows_out, rows_out), in_specs=[hbm] * 1...]
where the time goes in v3:
time: 109 us; the launch traced here: 108 us
  Pallas kernels  105 us (96%)
  local copies, waits for them, and re-layouts  2.64 us (2%)
    pallas_call x1, Pallas kernels, per_device(): pl.pallas_call(kernel, out_shape=(rows_out, rows_out), in_specs=[hbm] * 1...  105 us
    unnamed x4, local copies, waits for them, and re-layouts  2.64 us

profile of v3, /device:TPU:4, one launch (start us, length us, event | category | flops | bytes accessed | tf_op | source)
XLA Modules:
  0.0 107.8 jit_solution(16528087681511370532)
XLA Ops:
  0.6 104.5 %routed_experts.1 = (bf16[1,64,3584]{2,1,0:T(8,128)(2,1)}, bf16[1,64,3584]{2,1,0:T(8,128)(2,1)}) custom-call(bf16[1,64,3584]{2,1,0:T(8,128)(2,1)} %fi_in.1, s32[1,64]{1,0:T(1,128)} %bitcast.6, f32[1,64]{1,0:T(1,128)} %fw_in.1, bf16[1,64,3584]{2,1,0:T(8,128)(2,1)} %bg_in.1, s32[1,64]{1,0:T(1,128)} %bitcast.7, f32[1,64]{1,0:T(1,128)} %bw_in.1, ...), custom_call_target="tpu_custom_call" | custom-call | tf_op jit(solution)/shard_map/routed_experts/pallas_call | solution.py:422
  105.2 0.0 copy-start
  105.2 1.9 %copy.14 = bf16[1,64,3584]{2,1,0:T(8,128)(2,1)} copy(bf16[1,64,3584]{2,1,0:T(8,128)(2,1)} %get-tuple-element.4) | data formatting | bytes 917504
  107.0 0.0 copy-done
  107.0 0.8 copy.15
Async XLA Ops:
  105.2 1.9 %copy-start = (bf16[1,64,3584]{2,1,0:T(8,128)(2,1)S(1)}, bf16[1,64,3584]{2,1,0:T(8,128)(2,1)}, u32[]{:S(2)}) copy-start(bf16[1,64,3584]{2,1,0:T(8,128)(2,1)} %get-tuple-element.5) | copy-start | bytes 1376260

commit v4 on v3

--- a/solution.py
+++ b/solution.py
@@ -17,12 +17,12 @@
 HALF = BLK // 2
 WIDE = D + HALF
 TAIL = pl.ds(D, HALF)
-GROUPS = ((0, 2), (2, 4), (4, 6), (6, 7))
+GROUPS = ((0, 1), (1, 3), (3, 5), (5, 6), (6, 7))
 NG = len(GROUPS)
 FWD, BWD = 0, 1
 STEPS = (0, 2, 1, 3)
 W_FIRST = 2
-W_AHEAD = 4
+W_AHEAD = 5
 B_LAG = 2
 F_OWN_EARLY = True
 
@@ -212,8 +212,6 @@
             up.at[0, cols], uw.at[cols, pl.ds(UNITS, UNITS)],
             w_send.at[2 + NG + g], w_recv.at[2 + NG + g], weight_peer))
 
-    pl.semaphore_wait(barrier, len(peers))
-    from_down = remote(down.at[0], dw.at[pl.ds(UNITS, UNITS)], w_send.at[0], w_recv.at[0], weight_peer)
     for copy in small[:3]:
         copy.wait()
     index_b = row_index(column(br[...]))
@@ -223,6 +221,8 @@
     for g in range(NG):
         pick_main(BWD, lanes_b, read_grad, g)
     pick_extra(BWD, lanes_b, read_grad)
+    pl.semaphore_wait(barrier, len(peers))
+    from_down = remote(down.at[0], dw.at[pl.ds(UNITS, UNITS)], w_send.at[0], w_recv.at[0], weight_peer)
     for at in range(1, 4):
         send_rows(BWD, at)
     pass_rows(BWD, 0)
@@ -356,11 +356,10 @@
             send_sum(BWD, g - B_LAG, None)
     if not F_OWN_EARLY:
         pass_rows(FWD, 0)
-    pass_rows(FWD, 1)
+    for at in range(1, 4):
+        pass_rows(FWD, at)
     for g in range(max(NG - B_LAG, 0), NG):
         send_sum(BWD, g, None)
-    pass_rows(FWD, 2)
-    pass_rows(FWD, 3)
 
     for half in range(2):
         for at in (2 * half, 2 * half + 1):
@@ -416,7 +415,7 @@
     vmem = pl.BlockSpec(memory_space=pltpu.VMEM)
     hbm = pl.BlockSpec(memory_space=pltpu.HBM)
     dma = pltpu.SemaphoreType.DMA
-    rows_out = jax.ShapeDtypeStruct((1, TOK, D), BF16)
+    rows_out = pltpu.VMEM((1, TOK, D), BF16)
     saved = saved[0].transpose(0, 2, 1, 3)
     fr, br = fr.reshape(1, TOK), br.reshape(1, TOK)
     return pl.pallas_call(

time: 109 us -> 105 us (0.963)
  Pallas kernels: 105 us -> 103 us
  local copies, waits for them, and re-layouts: 2.64 us -> 1.54 us
    pallas_call x1, Pallas kernels: 105 us -> 103 us  [per_device(): pl.pallas_call(kernel, out_shape=(rows_out, rows_out), in_specs=[hbm] * 1...]
    unnamed x4 -> x2, local copies, waits for them, and re-layouts: 2.64 us -> 1.54 us
where the time goes in v4:
time: 105 us
  Pallas kernels  103 us (98%)
  local copies, waits for them, and re-layouts  1.54 us (1%)
    pallas_call x1, Pallas kernels, per_device(): pl.pallas_call(kernel, out_shape=(rows_out, rows_out), in_specs=[hbm] * 1...  103 us

profile of v4, /device:TPU:4, one launch (start us, length us, event | category | flops | bytes accessed | tf_op | source)
XLA Modules:
  0.0 104.7 jit_solution(15203828657901552500)
XLA Ops:
  0.6 102.6 %routed_experts.1 = (bf16[1,64,3584]{2,1,0:T(8,128)(2,1)S(1)}, bf16[1,64,3584]{2,1,0:T(8,128)(2,1)S(1)}) custom-call(bf16[1,64,3584]{2,1,0:T(8,128)(2,1)} %fi_in.1, s32[1,64]{1,0:T(1,128)} %bitcast.6, f32[1,64]{1,0:T(1,128)} %fw_in.1, bf16[1,64,3584]{2,1,0:T(8,128)(2,1)} %bg_in.1, s32[1,64]{1,0:T(1,128)} %bitcast.7, f32[1,64]{1,0:T(1,128)} %bw_in.1, ...), custom_call_target="tpu_custom_call" | custom-call | tf_op jit(solution)/shard_map/routed_experts/pallas_call | solution.py:421
  103.2 0.8 copy.14
  104.0 0.8 copy.15

commit v5 on v4

--- a/solution.py
+++ b/solution.py
@@ -376,6 +376,7 @@
             for c in range(*GROUPS[g]):
                 keep(FWD, c, dot(act_a[:144], dw[:, block_cols(c)]), half)
             send_part(FWD, g, half)
+        early = len(sends)
         for g in range(NG):
             send_sum(FWD, g, half)
 
@@ -406,8 +407,10 @@
             out[0, :, block_cols(c)] = value.astype(BF16)
 
     place(BWD, out_b)
+    for copy in sends[:early]:
+        copy.wait_send()
     place(FWD, out_f)
-    for copy in sends:
+    for copy in sends[early:]:
         copy.wait_send()
 
 

time: 105 us -> 105 us (level)
  no operation moved by 1% of the time
where the time goes in v5:
time: 105 us
  Pallas kernels  102 us (97%)
  local copies, waits for them, and re-layouts  1.54 us (1%)
    pallas_call x1, Pallas kernels, per_device(): pl.pallas_call(kernel, out_shape=(rows_out, rows_out), in_specs=[hbm] * 1...  102 us

profile of v5, /device:TPU:4, one launch (start us, length us, event | category | flops | bytes accessed | tf_op | source)
XLA Modules:
  0.0 104.6 jit_solution(6469844373493074309)
XLA Ops:
  0.6 102.4 %routed_experts.1 = (bf16[1,64,3584]{2,1,0:T(8,128)(2,1)S(1)}, bf16[1,64,3584]{2,1,0:T(8,128)(2,1)S(1)}) custom-call(bf16[1,64,3584]{2,1,0:T(8,128)(2,1)} %fi_in.1, s32[1,64]{1,0:T(1,128)} %bitcast.6, f32[1,64]{1,0:T(1,128)} %fw_in.1, bf16[1,64,3584]{2,1,0:T(8,128)(2,1)} %bg_in.1, s32[1,64]{1,0:T(1,128)} %bitcast.7, f32[1,64]{1,0:T(1,128)} %bw_in.1, ...), custom_call_target="tpu_custom_call" | custom-call | tf_op jit(solution)/shard_map/routed_experts/pallas_call | solution.py:424
  103.1 0.8 copy.14
  103.9 0.8 copy.15
